TPU v7x, 32 devices: a whole 2x2x4 slice. The times are simulated.
32 devices in a mesh: horiz: 8 (over z, y), vert: 4 (over x, core).
Axes of the slice: x: 2, y: 2, z: 4, core: 2. Of those that a mesh axis runs over, the one named last changes fastest.
Arguments:
- tracer: bfloat16 [8, 2048, 128], P('vert', 'horiz'), may hold values from -6 to 6
- explicit_tiles: bfloat16 [8, 16, 7, 128, 128], P('vert', 'horiz'), may hold values from -0.25 to 0.25
- tile_columns: int32 [8, 16, 7], P('vert', 'horiz'), may hold values from 0 to 127, as said below
- tile_counts: int32 [8, 16], P('vert', 'horiz'), may hold values from 4 to 7
- surface_source: bfloat16 [2048, 128], P('horiz'), may hold values from -6 to 6
- implicit_columns: float32 [2048, 8, 8], P(('horiz', 'vert')), may hold values from -0.53033009 to 1
- settling: float32 [128], replicated, may hold values from 0.02 to 0.5
- wet_mask: int32 [8, 2048], P('vert', 'horiz'), may hold values 0 or 1
Outputs:
- tracer_out: bfloat16 [8, 2048, 128], P('vert', 'horiz')
Inputs may be any that keep to these rules, and one draw needn't show every extreme that they name: `tile_columns`: slot 0 of block row (l, t) names the row's own tile l * 16 + t; the other slots name distinct tiles within 2 levels and 2 tiles of it, inside the grid.
All inputs are finite; a program needn't handle non-finite values. No bound on the sum of `wet_mask` on one device may be relied on, other than what follows from the above.
Results may differ from a plain program's by a relative error of at most 0.015.
Values may be sent and summed in bfloat16 or wider, within the bound.
A program may use at most 64 MiB of HBM per device.

v0:
```python
import jax
import jax.numpy as jnp
from jax import lax
from jax.sharding import PartitionSpec as P

REACH = 2
STEPS = 4


def extended(shard, sides, width):
    for axis, dim in sides:
        size, length = (lax.axis_size(axis), shard.shape[dim])
        up = [(i, (i + 1) % size) for i in range(size - 1)]
        down = [(j, i) for i, j in up]
        last = lax.slice_in_dim(shard, length - width, length, axis=dim)
        leading = lax.slice_in_dim(shard, 0, width, axis=dim)
        before = lax.ppermute(last, axis, up)
        after = lax.ppermute(leading, axis, down)
        shard = jnp.concatenate([before, shard, after], axis=dim)
    return shard


def from_behind(value, axis, steps):
    count = lax.axis_size(axis)
    leading, last = (max(0, -steps), min(count, count - steps))
    return lax.ppermute(value, axis, [(source, source + steps) for source in range(leading, last)])


def on_device(
    tracer,
    explicit_tiles,
    tile_columns,
    tile_counts,
    surface_source,
    implicit_columns,
    settling,
    wet_mask,
):
    lev_dev, cells_dev, classes = tracer.shape
    tile_size = explicit_tiles.shape[-1]
    tiles_dev = cells_dev // tile_size
    slot_count = explicit_tiles.shape[2]
    h_tiles = tiles_dev * lax.axis_size("horiz")
    wide_tiles = tiles_dev + 2 * REACH
    first_level = lax.axis_index("vert") * lev_dev
    first_tile = lax.axis_index("horiz") * tiles_dev
    col_level = tile_columns // h_tiles - (first_level - REACH)
    col_tile = tile_columns % h_tiles - (first_tile - REACH)
    position = col_level * wide_tiles + col_tile
    live_slots = (
        jnp.arange(slot_count, dtype=jnp.int32)[None, None, :] < tile_counts[:, :, None]
    ).astype(jnp.bfloat16)
    on_top = first_level + jnp.arange(lev_dev, dtype=jnp.int32) == 0
    source = surface_source.astype(jnp.float32)
    fall_rate = settling[None, None, :]
    wet_cells = wet_mask.astype(jnp.bfloat16)[:, :, None]
    all_columns = lax.all_gather(implicit_columns, "vert", axis=0, tiled=True)
    own_rows = lax.dynamic_slice_in_dim(all_columns, first_level, lev_dev, 1)
    current = tracer
    for step_index in range(STEPS):
        slab_grid = current.reshape(lev_dev, tiles_dev, tile_size, classes)
        padded = extended(slab_grid, (("horiz", 1), ("vert", 0)), REACH)
        flattened = padded.reshape(-1, tile_size, classes)
        picked = flattened[position] * live_slots[:, :, :, None, None]
        explicit_flow = jnp.einsum(
            "ltjab,ltjbs->ltas", explicit_tiles, picked, preferred_element_type=jnp.float32
        )
        explicit_flow = explicit_flow.reshape(lev_dev, cells_dev, classes)
        explicit_flow = explicit_flow + jnp.where(on_top[:, None, None], source[None, :, :], 0.0)
        loaded = explicit_flow.astype(jnp.bfloat16)
        mixed_col = jnp.einsum(
            "ckm,mcs->kcs",
            own_rows,
            lax.all_gather(loaded, "vert", axis=0, tiled=True).astype(jnp.float32),
            precision=lax.Precision.HIGHEST,
        )
        upper_level = from_behind(mixed_col[-1].astype(jnp.bfloat16), "vert", 1).astype(jnp.float32)
        from_above = jnp.concatenate([upper_level[None], mixed_col[:-1]], axis=0)
        settled = (1.0 - fall_rate) * mixed_col + fall_rate * from_above
        current = (settled * wet_cells.astype(jnp.float32)).astype(jnp.bfloat16)
    return current


def solution(mesh):
    placed = (
        P("vert", "horiz", None),
        P("vert", "horiz", None, None, None),
        P("vert", "horiz", None),
        P("vert", "horiz"),
        P("horiz", None),
        P(("horiz", "vert"), None, None),
        P(),
        P("vert", "horiz"),
    )
    return jax.shard_map(
        on_device, mesh=mesh, in_specs=placed, out_specs=P("vert", "horiz", None), check_vma=False
    )
```

profile of v0, /device:TPU:1, one launch (start us, length us, event | category | flops | bytes accessed | tf_op | source)
XLA Modules:
  0.0 167.6 jit_solution(6005104641196930024)
XLA Ops:
  1.4 4.6 %collective-permute-start = (bf16[2,2,128,128]{3,2,1,0:T(8,128)(2,1)}, bf16[2,2,128,128]{3,2,1,0:T(8,128)(2,1)S(1)}, u32[]{:S(2)}, u32[]{:S(2)}) collective-permute-start(bf16[2,2,128,128]{3,2,1,0:T(8,128)(2,1)} %bitcast.83), channel_id=1, source_target_pairs={{0,4},{4,8},{8,12},{12,16},{16,20},{20,24},{24,28},{1,5},{5,9},{9,... | collective-permute-start | bytes 393224 | tf_op jit(solution)/shard_map/ppermute | solution.py:17
  8.7 11.3 %all_gather.16 = f32[256,8,8]{2,1,0:T(8,128)S(1)} all-gather(f32[64,8,8]{2,1,0:T(8,128)S(1)} %copy.38), channel_id=1, replica_groups=mesh['horiz'=8,'vert'=4] {'vert'}, dimensions={0}, use_global_device_ids=true | all-gather | bytes 81920 | tf_op jit(solution)/shard_map/all_gather | solution.py:57
  20.1 2.1 %collective-permute-start.3 = (bf16[2,6,128,128]{3,2,1,0:T(8,128)(2,1)S(1)}, bf16[2,6,128,128]{3,2,1,0:T(8,128)(2,1)S(1)}, u32[]{:S(2)}, u32[]{:S(2)}) collective-permute-start(bf16[2,6,128,128]{3,2,1,0:T(8,128)(2,1)S(1)} %pad_maximum_fusion.4), channel_id=1, source_target_pairs={{1,0},{2,1},{3,2},{5,4},{6,5},{7,6},{9,8},{10,9},{11,10},{13,12},{... | collective-permute-start | bytes 1179656 | tf_op jit(solution)/shard_map/ppermute | solution.py:18
  22.1 3.5 %collective-permute-start.2 = (bf16[2,6,128,128]{3,2,1,0:T(8,128)(2,1)S(1)}, bf16[2,6,128,128]{3,2,1,0:T(8,128)(2,1)S(1)}, u32[]{:S(2)}, u32[]{:S(2)}) collective-permute-start(bf16[2,6,128,128]{3,2,1,0:T(8,128)(2,1)S(1)} %pad_maximum_fusion.4), channel_id=1, source_target_pairs={{0,1},{1,2},{2,3},{4,5},{5,6},{6,7},{8,9},{9,10},{10,11},{12,13},{... | collective-permute-start | bytes 1179656 | tf_op jit(solution)/shard_map/ppermute | solution.py:17
  25.7 3.4 %collective-permute-done.3 = bf16[2,6,128,128]{3,2,1,0:T(8,128)(2,1)S(1)} collective-permute-done((bf16[2,6,128,128]{3,2,1,0:T(8,128)(2,1)S(1)}, bf16[2,6,128,128]{3,2,1,0:T(8,128)(2,1)S(1)}, u32[]{:S(2)}, u32[]{:S(2)}) %collective-permute-start.3) | collective-permute-done | bytes 393248 | tf_op jit(solution)/shard_map/ppermute | solution.py:18
  34.8 8.4 %all_gather.15 = bf16[8,256,128]{2,1,0:T(8,128)(2,1)S(1)} all-gather(bf16[2,256,128]{2,1,0:T(8,128)(2,1)S(1)} %fusion.16), channel_id=1, replica_groups=mesh['horiz'=8,'vert'=4] {'vert'}, dimensions={0}, use_global_device_ids=true | all-gather | bytes 655360 | tf_op jit(solution)/shard_map/all_gather | solution.py:74
  44.6 2.5 %collective-permute-start.4 = (bf16[256,128]{1,0:T(8,128)(2,1)S(1)}, bf16[256,128]{1,0:T(8,128)(2,1)S(1)}, u32[]{:S(2)}, u32[]{:S(2)}) collective-permute-start(bf16[256,128]{1,0:T(8,128)(2,1)S(1)} %bitcast.90), channel_id=1, source_target_pairs={{0,1},{1,2},{2,3},{4,5},{5,6},{6,7},{8,9},{9,10},{10,11},{12,13},{... | collective-permute-start | bytes 196616 | tf_op jit(solution)/shard_map/ppermute | solution.py:26
  48.8 4.0 %collective-permute-start.5 = (bf16[2,2,128,128]{3,2,1,0:T(8,128)(2,1)S(1)}, bf16[2,2,128,128]{3,2,1,0:T(8,128)(2,1)S(1)}, u32[]{:S(2)}, u32[]{:S(2)}) collective-permute-start(bf16[2,2,128,128]{3,2,1,0:T(8,128)(2,1)S(1)} %copy.42), channel_id=1, source_target_pairs={{0,4},{4,8},{8,12},{12,16},{16,20},{20,24},{24,28},{1,5},{5,9},{9,... | collective-permute-start | bytes 393224 | tf_op jit(solution)/shard_map/ppermute | solution.py:17
  54.2 2.0 %collective-permute-done.5 = bf16[2,2,128,128]{3,2,1,0:T(8,128)(2,1)S(1)} collective-permute-done((bf16[2,2,128,128]{3,2,1,0:T(8,128)(2,1)S(1)}, bf16[2,2,128,128]{3,2,1,0:T(8,128)(2,1)S(1)}, u32[]{:S(2)}, u32[]{:S(2)}) %collective-permute-start.5) | collective-permute-done | bytes 131104 | tf_op jit(solution)/shard_map/ppermute | solution.py:17
  56.2 3.8 %collective-permute-done.6 = bf16[2,2,128,128]{3,2,1,0:T(8,128)(2,1)S(1)} collective-permute-done((bf16[2,2,128,128]{3,2,1,0:T(8,128)(2,1)S(1)}, bf16[2,2,128,128]{3,2,1,0:T(8,128)(2,1)S(1)}, u32[]{:S(2)}, u32[]{:S(2)}) %collective-permute-start.6) | collective-permute-done | bytes 131104 | tf_op jit(solution)/shard_map/ppermute | solution.py:18
  60.1 2.5 %collective-permute-start.8 = (bf16[2,6,128,128]{3,2,1,0:T(8,128)(2,1)S(1)}, bf16[2,6,128,128]{3,2,1,0:T(8,128)(2,1)S(1)}, u32[]{:S(2)}, u32[]{:S(2)}) collective-permute-start(bf16[2,6,128,128]{3,2,1,0:T(8,128)(2,1)S(1)} %constant_dynamic-update-slice_fusion), channel_id=1, source_target_pairs={{1,0},{2,1},{3,2},{5,4},{6,5},{7,6},{9,8},{10,9},{11,10},{13,12},{... | collective-permute-start | bytes 1179656 | tf_op jit(solution)/shard_map/ppermute | solution.py:18
  62.6 3.6 %collective-permute-start.7 = (bf16[2,6,128,128]{3,2,1,0:T(8,128)(2,1)S(1)}, bf16[2,6,128,128]{3,2,1,0:T(8,128)(2,1)S(1)}, u32[]{:S(2)}, u32[]{:S(2)}) collective-permute-start(bf16[2,6,128,128]{3,2,1,0:T(8,128)(2,1)S(1)} %constant_dynamic-update-slice_fusion), channel_id=1, source_target_pairs={{0,1},{1,2},{2,3},{4,5},{5,6},{6,7},{8,9},{9,10},{10,11},{12,13},{... | collective-permute-start | bytes 1179656 | tf_op jit(solution)/shard_map/ppermute | solution.py:17
  66.2 3.5 %collective-permute-done.8 = bf16[2,6,128,128]{3,2,1,0:T(8,128)(2,1)S(1)} collective-permute-done((bf16[2,6,128,128]{3,2,1,0:T(8,128)(2,1)S(1)}, bf16[2,6,128,128]{3,2,1,0:T(8,128)(2,1)S(1)}, u32[]{:S(2)}, u32[]{:S(2)}) %collective-permute-start.8) | collective-permute-done | bytes 393248 | tf_op jit(solution)/shard_map/ppermute | solution.py:18
  74.5 8.4 %all_gather.17 = bf16[8,256,128]{2,1,0:T(8,128)(2,1)S(1)} all-gather(bf16[2,256,128]{2,1,0:T(8,128)(2,1)S(1)} %fusion.17), channel_id=1, replica_groups=mesh['horiz'=8,'vert'=4] {'vert'}, dimensions={0}, use_global_device_ids=true | all-gather | bytes 655360 | tf_op jit(solution)/shard_map/all_gather | solution.py:74
  84.2 2.5 %collective-permute-start.9 = (bf16[256,128]{1,0:T(8,128)(2,1)S(1)}, bf16[256,128]{1,0:T(8,128)(2,1)S(1)}, u32[]{:S(2)}, u32[]{:S(2)}) collective-permute-start(bf16[256,128]{1,0:T(8,128)(2,1)S(1)} %bitcast.91), channel_id=1, source_target_pairs={{0,1},{1,2},{2,3},{4,5},{5,6},{6,7},{8,9},{9,10},{10,11},{12,13},{... | collective-permute-start | bytes 196616 | tf_op jit(solution)/shard_map/ppermute | solution.py:26
  88.5 3.1 %collective-permute-start.10 = (bf16[2,2,128,128]{3,2,1,0:T(8,128)(2,1)S(1)}, bf16[2,2,128,128]{3,2,1,0:T(8,128)(2,1)S(1)}, u32[]{:S(2)}, u32[]{:S(2)}) collective-permute-start(bf16[2,2,128,128]{3,2,1,0:T(8,128)(2,1)S(1)} %copy.47), channel_id=1, source_target_pairs={{0,4},{4,8},{8,12},{12,16},{16,20},{20,24},{24,28},{1,5},{5,9},{9,... | collective-permute-start | bytes 393224 | tf_op jit(solution)/shard_map/ppermute | solution.py:17
  92.9 2.0 %collective-permute-done.10 = bf16[2,2,128,128]{3,2,1,0:T(8,128)(2,1)S(1)} collective-permute-done((bf16[2,2,128,128]{3,2,1,0:T(8,128)(2,1)S(1)}, bf16[2,2,128,128]{3,2,1,0:T(8,128)(2,1)S(1)}, u32[]{:S(2)}, u32[]{:S(2)}) %collective-permute-start.10) | collective-permute-done | bytes 131104 | tf_op jit(solution)/shard_map/ppermute | solution.py:17
  95.0 3.8 %collective-permute-done.11 = bf16[2,2,128,128]{3,2,1,0:T(8,128)(2,1)S(1)} collective-permute-done((bf16[2,2,128,128]{3,2,1,0:T(8,128)(2,1)S(1)}, bf16[2,2,128,128]{3,2,1,0:T(8,128)(2,1)S(1)}, u32[]{:S(2)}, u32[]{:S(2)}) %collective-permute-start.11) | collective-permute-done | bytes 131104 | tf_op jit(solution)/shard_map/ppermute | solution.py:18
  98.8 2.5 %collective-permute-start.13 = (bf16[2,6,128,128]{3,2,1,0:T(8,128)(2,1)S(1)}, bf16[2,6,128,128]{3,2,1,0:T(8,128)(2,1)S(1)}, u32[]{:S(2)}, u32[]{:S(2)}) collective-permute-start(bf16[2,6,128,128]{3,2,1,0:T(8,128)(2,1)S(1)} %constant_dynamic-update-slice_fusion.3), channel_id=1, source_target_pairs={{1,0},{2,1},{3,2},{5,4},{6,5},{7,6},{9,8},{10,9},{11,10},{13,12},{... | collective-permute-start | bytes 1179656 | tf_op jit(solution)/shard_map/ppermute | solution.py:18
  101.4 3.6 %collective-permute-start.12 = (bf16[2,6,128,128]{3,2,1,0:T(8,128)(2,1)S(1)}, bf16[2,6,128,128]{3,2,1,0:T(8,128)(2,1)S(1)}, u32[]{:S(2)}, u32[]{:S(2)}) collective-permute-start(bf16[2,6,128,128]{3,2,1,0:T(8,128)(2,1)S(1)} %constant_dynamic-update-slice_fusion.3), channel_id=1, source_target_pairs={{0,1},{1,2},{2,3},{4,5},{5,6},{6,7},{8,9},{9,10},{10,11},{12,13},{... | collective-permute-start | bytes 1179656 | tf_op jit(solution)/shard_map/ppermute | solution.py:17
  105.0 3.5 %collective-permute-done.13 = bf16[2,6,128,128]{3,2,1,0:T(8,128)(2,1)S(1)} collective-permute-done((bf16[2,6,128,128]{3,2,1,0:T(8,128)(2,1)S(1)}, bf16[2,6,128,128]{3,2,1,0:T(8,128)(2,1)S(1)}, u32[]{:S(2)}, u32[]{:S(2)}) %collective-permute-start.13) | collective-permute-done | bytes 393248 | tf_op jit(solution)/shard_map/ppermute | solution.py:18
  111.5 1.7 fusion.2
  113.2 8.4 %all_gather.18 = bf16[8,256,128]{2,1,0:T(8,128)(2,1)S(1)} all-gather(bf16[2,256,128]{2,1,0:T(8,128)(2,1)S(1)} %fusion.18), channel_id=1, replica_groups=mesh['horiz'=8,'vert'=4] {'vert'}, dimensions={0}, use_global_device_ids=true | all-gather | bytes 655360 | tf_op jit(solution)/shard_map/all_gather | solution.py:74
  123.0 2.5 %collective-permute-start.14 = (bf16[256,128]{1,0:T(8,128)(2,1)S(1)}, bf16[256,128]{1,0:T(8,128)(2,1)S(1)}, u32[]{:S(2)}, u32[]{:S(2)}) collective-permute-start(bf16[256,128]{1,0:T(8,128)(2,1)S(1)} %bitcast.92), channel_id=1, source_target_pairs={{0,1},{1,2},{2,3},{4,5},{5,6},{6,7},{8,9},{9,10},{10,11},{12,13},{... | collective-permute-start | bytes 196616 | tf_op jit(solution)/shard_map/ppermute | solution.py:26
  127.2 4.1 %collective-permute-start.15 = (bf16[2,2,128,128]{3,2,1,0:T(8,128)(2,1)S(1)}, bf16[2,2,128,128]{3,2,1,0:T(8,128)(2,1)S(1)}, u32[]{:S(2)}, u32[]{:S(2)}) collective-permute-start(bf16[2,2,128,128]{3,2,1,0:T(8,128)(2,1)S(1)} %copy.51), channel_id=1, source_target_pairs={{0,4},{4,8},{8,12},{12,16},{16,20},{20,24},{24,28},{1,5},{5,9},{9,... | collective-permute-start | bytes 393224 | tf_op jit(solution)/shard_map/ppermute | solution.py:17
  132.6 2.0 %collective-permute-done.15 = bf16[2,2,128,128]{3,2,1,0:T(8,128)(2,1)S(1)} collective-permute-done((bf16[2,2,128,128]{3,2,1,0:T(8,128)(2,1)S(1)}, bf16[2,2,128,128]{3,2,1,0:T(8,128)(2,1)S(1)}, u32[]{:S(2)}, u32[]{:S(2)}) %collective-permute-start.15) | collective-permute-done | bytes 131104 | tf_op jit(solution)/shard_map/ppermute | solution.py:17
  134.6 3.8 %collective-permute-done.16 = bf16[2,2,128,128]{3,2,1,0:T(8,128)(2,1)S(1)} collective-permute-done((bf16[2,2,128,128]{3,2,1,0:T(8,128)(2,1)S(1)}, bf16[2,2,128,128]{3,2,1,0:T(8,128)(2,1)S(1)}, u32[]{:S(2)}, u32[]{:S(2)}) %collective-permute-start.16) | collective-permute-done | bytes 131104 | tf_op jit(solution)/shard_map/ppermute | solution.py:18
  138.5 2.5 %collective-permute-start.18 = (bf16[2,6,128,128]{3,2,1,0:T(8,128)(2,1)S(1)}, bf16[2,6,128,128]{3,2,1,0:T(8,128)(2,1)S(1)}, u32[]{:S(2)}, u32[]{:S(2)}) collective-permute-start(bf16[2,6,128,128]{3,2,1,0:T(8,128)(2,1)S(1)} %constant_dynamic-update-slice_fusion.6), channel_id=1, source_target_pairs={{1,0},{2,1},{3,2},{5,4},{6,5},{7,6},{9,8},{10,9},{11,10},{13,12},{... | collective-permute-start | bytes 1179656 | tf_op jit(solution)/shard_map/ppermute | solution.py:18
  141.0 3.8 %collective-permute-start.17 = (bf16[2,6,128,128]{3,2,1,0:T(8,128)(2,1)S(1)}, bf16[2,6,128,128]{3,2,1,0:T(8,128)(2,1)S(1)}, u32[]{:S(2)}, u32[]{:S(2)}) collective-permute-start(bf16[2,6,128,128]{3,2,1,0:T(8,128)(2,1)S(1)} %constant_dynamic-update-slice_fusion.6), channel_id=1, source_target_pairs={{0,1},{1,2},{2,3},{4,5},{5,6},{6,7},{8,9},{9,10},{10,11},{12,13},{... | collective-permute-start | bytes 1179656 | tf_op jit(solution)/shard_map/ppermute | solution.py:17
  144.9 3.3 %collective-permute-done.18 = bf16[2,6,128,128]{3,2,1,0:T(8,128)(2,1)S(1)} collective-permute-done((bf16[2,6,128,128]{3,2,1,0:T(8,128)(2,1)S(1)}, bf16[2,6,128,128]{3,2,1,0:T(8,128)(2,1)S(1)}, u32[]{:S(2)}, u32[]{:S(2)}) %collective-permute-start.18) | collective-permute-done | bytes 393248 | tf_op jit(solution)/shard_map/ppermute | solution.py:18
  152.9 8.4 %all_gather.19 = bf16[8,256,128]{2,1,0:T(8,128)(2,1)S(1)} all-gather(bf16[2,256,128]{2,1,0:T(8,128)(2,1)S(1)} %fusion.19), channel_id=1, replica_groups=mesh['horiz'=8,'vert'=4] {'vert'}, dimensions={0}, use_global_device_ids=true | all-gather | bytes 655360 | tf_op jit(solution)/shard_map/all_gather | solution.py:74
  162.7 2.5 %collective-permute-start.19 = (bf16[256,128]{1,0:T(8,128)(2,1)S(1)}, bf16[256,128]{1,0:T(8,128)(2,1)S(1)}, u32[]{:S(2)}, u32[]{:S(2)}) collective-permute-start(bf16[256,128]{1,0:T(8,128)(2,1)S(1)} %bitcast.93), channel_id=1, source_target_pairs={{0,1},{1,2},{2,3},{4,5},{5,6},{6,7},{8,9},{9,10},{10,11},{12,13},{... | collective-permute-start | bytes 196616 | tf_op jit(solution)/shard_map/ppermute | solution.py:26
  (89 shorter events, 39.1 us)
Async XLA Ops:
  0.0 33.0 %copy-start = (bf16[2,2,7,128,128]{4,3,2,1,0:T(8,128)(2,1)S(1)}, bf16[2,2,7,128,128]{4,3,2,1,0:T(8,128)(2,1)}, u32[]{:S(2)}) copy-start(bf16[2,2,7,128,128]{4,3,2,1,0:T(8,128)(2,1)} %param.9) | copy-start | bytes 2752516
  0.0 20.0 %copy-start.1 = (bf16[2,256,128]{2,1,0:T(8,128)(2,1)S(1)}, bf16[2,256,128]{2,1,0:T(8,128)(2,1)}, u32[]{:S(2)}) copy-start(bf16[2,256,128]{2,1,0:T(8,128)(2,1)} %param.8) | copy-start | bytes 393220
  0.0 20.0 %collective-permute-start.1 = (bf16[2,2,128,128]{3,2,1,0:T(8,128)(2,1)}, bf16[2,2,128,128]{3,2,1,0:T(8,128)(2,1)S(1)}, u32[]{:S(2)}, u32[]{:S(2)}) collective-permute-start(bf16[2,2,128,128]{3,2,1,0:T(8,128)(2,1)} %bitcast.82), channel_id=1, source_target_pairs={{4,0},{8,4},{12,8},{16,12},{20,16},{24,20},{28,24},{5,1},{9,5},{13... | collective-permute-start | bytes 393224 | tf_op jit(solution)/shard_map/ppermute | solution.py:18
  1.4 18.6 %collective-permute-start = (bf16[2,2,128,128]{3,2,1,0:T(8,128)(2,1)}, bf16[2,2,128,128]{3,2,1,0:T(8,128)(2,1)S(1)}, u32[]{:S(2)}, u32[]{:S(2)}) collective-permute-start(bf16[2,2,128,128]{3,2,1,0:T(8,128)(2,1)} %bitcast.83), channel_id=1, source_target_pairs={{0,4},{4,8},{8,12},{12,16},{16,20},{20,24},{24,28},{1,5},{5,9},{9,... | collective-permute-start | bytes 393224 | tf_op jit(solution)/shard_map/ppermute | solution.py:17
  7.7 17.9 %copy-start.5 = (s32[2,2]{1,0:T(2,128)S(1)}, s32[2,2]{1,0:T(2,128)}, u32[]{:S(2)}) copy-start(s32[2,2]{1,0:T(2,128)} %param.11) | copy-start | bytes 52
  7.7 18.0 %copy-start.4 = (s32[2,256]{1,0:T(2,128)S(1)}, s32[2,256]{1,0:T(2,128)}, u32[]{:S(2)}) copy-start(s32[2,256]{1,0:T(2,128)} %param.15) | copy-start | bytes 6148
  20.0 9.2 %copy-start.2 = (bf16[2,2,128,128]{3,2,1,0:T(8,128)(2,1)}, bf16[2,2,128,128]{3,2,1,0:T(8,128)(2,1)S(1)}, u32[]{:S(2)}) copy-start(bf16[2,2,128,128]{3,2,1,0:T(8,128)(2,1)S(1)} %collective-permute-done) | copy-start | bytes 393220
  20.1 9.1 %collective-permute-start.3 = (bf16[2,6,128,128]{3,2,1,0:T(8,128)(2,1)S(1)}, bf16[2,6,128,128]{3,2,1,0:T(8,128)(2,1)S(1)}, u32[]{:S(2)}, u32[]{:S(2)}) collective-permute-start(bf16[2,6,128,128]{3,2,1,0:T(8,128)(2,1)S(1)} %pad_maximum_fusion.4), channel_id=1, source_target_pairs={{1,0},{2,1},{3,2},{5,4},{6,5},{7,6},{9,8},{10,9},{11,10},{13,12},{... | collective-permute-start | bytes 1179656 | tf_op jit(solution)/shard_map/ppermute | solution.py:18
  22.1 8.2 %collective-permute-start.2 = (bf16[2,6,128,128]{3,2,1,0:T(8,128)(2,1)S(1)}, bf16[2,6,128,128]{3,2,1,0:T(8,128)(2,1)S(1)}, u32[]{:S(2)}, u32[]{:S(2)}) collective-permute-start(bf16[2,6,128,128]{3,2,1,0:T(8,128)(2,1)S(1)} %pad_maximum_fusion.4), channel_id=1, source_target_pairs={{0,1},{1,2},{2,3},{4,5},{5,6},{6,7},{8,9},{9,10},{10,11},{12,13},{... | collective-permute-start | bytes 1179656 | tf_op jit(solution)/shard_map/ppermute | solution.py:17
  34.8 12.3 %copy-start.3 = (f32[128]{0:T(128)S(1)}, f32[128]{0:T(128)}, u32[]{:S(2)}) copy-start(f32[128]{0:T(128)} %param.14) | copy-start | bytes 1540
  44.6 3.8 %collective-permute-start.4 = (bf16[256,128]{1,0:T(8,128)(2,1)S(1)}, bf16[256,128]{1,0:T(8,128)(2,1)S(1)}, u32[]{:S(2)}, u32[]{:S(2)}) collective-permute-start(bf16[256,128]{1,0:T(8,128)(2,1)S(1)} %bitcast.90), channel_id=1, source_target_pairs={{0,1},{1,2},{2,3},{4,5},{5,6},{6,7},{8,9},{9,10},{10,11},{12,13},{... | collective-permute-start | bytes 196616 | tf_op jit(solution)/shard_map/ppermute | solution.py:26
  48.8 7.3 %collective-permute-start.5 = (bf16[2,2,128,128]{3,2,1,0:T(8,128)(2,1)S(1)}, bf16[2,2,128,128]{3,2,1,0:T(8,128)(2,1)S(1)}, u32[]{:S(2)}, u32[]{:S(2)}) collective-permute-start(bf16[2,2,128,128]{3,2,1,0:T(8,128)(2,1)S(1)} %copy.42), channel_id=1, source_target_pairs={{0,4},{4,8},{8,12},{12,16},{16,20},{20,24},{24,28},{1,5},{5,9},{9,... | collective-permute-start | bytes 393224 | tf_op jit(solution)/shard_map/ppermute | solution.py:17
  52.9 7.2 %collective-permute-start.6 = (bf16[2,2,128,128]{3,2,1,0:T(8,128)(2,1)S(1)}, bf16[2,2,128,128]{3,2,1,0:T(8,128)(2,1)S(1)}, u32[]{:S(2)}, u32[]{:S(2)}) collective-permute-start(bf16[2,2,128,128]{3,2,1,0:T(8,128)(2,1)S(1)} %copy.42), channel_id=1, source_target_pairs={{4,0},{8,4},{12,8},{16,12},{20,16},{24,20},{28,24},{5,1},{9,5},{13... | collective-permute-start | bytes 393224 | tf_op jit(solution)/shard_map/ppermute | solution.py:18
  60.1 9.7 %collective-permute-start.8 = (bf16[2,6,128,128]{3,2,1,0:T(8,128)(2,1)S(1)}, bf16[2,6,128,128]{3,2,1,0:T(8,128)(2,1)S(1)}, u32[]{:S(2)}, u32[]{:S(2)}) collective-permute-start(bf16[2,6,128,128]{3,2,1,0:T(8,128)(2,1)S(1)} %constant_dynamic-update-slice_fusion), channel_id=1, source_target_pairs={{1,0},{2,1},{3,2},{5,4},{6,5},{7,6},{9,8},{10,9},{11,10},{13,12},{... | collective-permute-start | bytes 1179656 | tf_op jit(solution)/shard_map/ppermute | solution.py:18
  62.6 8.3 %collective-permute-start.7 = (bf16[2,6,128,128]{3,2,1,0:T(8,128)(2,1)S(1)}, bf16[2,6,128,128]{3,2,1,0:T(8,128)(2,1)S(1)}, u32[]{:S(2)}, u32[]{:S(2)}) collective-permute-start(bf16[2,6,128,128]{3,2,1,0:T(8,128)(2,1)S(1)} %constant_dynamic-update-slice_fusion), channel_id=1, source_target_pairs={{0,1},{1,2},{2,3},{4,5},{5,6},{6,7},{8,9},{9,10},{10,11},{12,13},{... | collective-permute-start | bytes 1179656 | tf_op jit(solution)/shard_map/ppermute | solution.py:17
  84.2 3.8 %collective-permute-start.9 = (bf16[256,128]{1,0:T(8,128)(2,1)S(1)}, bf16[256,128]{1,0:T(8,128)(2,1)S(1)}, u32[]{:S(2)}, u32[]{:S(2)}) collective-permute-start(bf16[256,128]{1,0:T(8,128)(2,1)S(1)} %bitcast.91), channel_id=1, source_target_pairs={{0,1},{1,2},{2,3},{4,5},{5,6},{6,7},{8,9},{9,10},{10,11},{12,13},{... | collective-permute-start | bytes 196616 | tf_op jit(solution)/shard_map/ppermute | solution.py:26
  88.5 6.4 %collective-permute-start.10 = (bf16[2,2,128,128]{3,2,1,0:T(8,128)(2,1)S(1)}, bf16[2,2,128,128]{3,2,1,0:T(8,128)(2,1)S(1)}, u32[]{:S(2)}, u32[]{:S(2)}) collective-permute-start(bf16[2,2,128,128]{3,2,1,0:T(8,128)(2,1)S(1)} %copy.47), channel_id=1, source_target_pairs={{0,4},{4,8},{8,12},{12,16},{16,20},{20,24},{24,28},{1,5},{5,9},{9,... | collective-permute-start | bytes 393224 | tf_op jit(solution)/shard_map/ppermute | solution.py:17
  91.6 7.2 %collective-permute-start.11 = (bf16[2,2,128,128]{3,2,1,0:T(8,128)(2,1)S(1)}, bf16[2,2,128,128]{3,2,1,0:T(8,128)(2,1)S(1)}, u32[]{:S(2)}, u32[]{:S(2)}) collective-permute-start(bf16[2,2,128,128]{3,2,1,0:T(8,128)(2,1)S(1)} %copy.47), channel_id=1, source_target_pairs={{4,0},{8,4},{12,8},{16,12},{20,16},{24,20},{28,24},{5,1},{9,5},{13... | collective-permute-start | bytes 393224 | tf_op jit(solution)/shard_map/ppermute | solution.py:18
  98.8 9.7 %collective-permute-start.13 = (bf16[2,6,128,128]{3,2,1,0:T(8,128)(2,1)S(1)}, bf16[2,6,128,128]{3,2,1,0:T(8,128)(2,1)S(1)}, u32[]{:S(2)}, u32[]{:S(2)}) collective-permute-start(bf16[2,6,128,128]{3,2,1,0:T(8,128)(2,1)S(1)} %constant_dynamic-update-slice_fusion.3), channel_id=1, source_target_pairs={{1,0},{2,1},{3,2},{5,4},{6,5},{7,6},{9,8},{10,9},{11,10},{13,12},{... | collective-permute-start | bytes 1179656 | tf_op jit(solution)/shard_map/ppermute | solution.py:18
  101.4 8.3 %collective-permute-start.12 = (bf16[2,6,128,128]{3,2,1,0:T(8,128)(2,1)S(1)}, bf16[2,6,128,128]{3,2,1,0:T(8,128)(2,1)S(1)}, u32[]{:S(2)}, u32[]{:S(2)}) collective-permute-start(bf16[2,6,128,128]{3,2,1,0:T(8,128)(2,1)S(1)} %constant_dynamic-update-slice_fusion.3), channel_id=1, source_target_pairs={{0,1},{1,2},{2,3},{4,5},{5,6},{6,7},{8,9},{9,10},{10,11},{12,13},{... | collective-permute-start | bytes 1179656 | tf_op jit(solution)/shard_map/ppermute | solution.py:17
  123.0 3.8 %collective-permute-start.14 = (bf16[256,128]{1,0:T(8,128)(2,1)S(1)}, bf16[256,128]{1,0:T(8,128)(2,1)S(1)}, u32[]{:S(2)}, u32[]{:S(2)}) collective-permute-start(bf16[256,128]{1,0:T(8,128)(2,1)S(1)} %bitcast.92), channel_id=1, source_target_pairs={{0,1},{1,2},{2,3},{4,5},{5,6},{6,7},{8,9},{9,10},{10,11},{12,13},{... | collective-permute-start | bytes 196616 | tf_op jit(solution)/shard_map/ppermute | solution.py:26
  127.2 7.3 %collective-permute-start.15 = (bf16[2,2,128,128]{3,2,1,0:T(8,128)(2,1)S(1)}, bf16[2,2,128,128]{3,2,1,0:T(8,128)(2,1)S(1)}, u32[]{:S(2)}, u32[]{:S(2)}) collective-permute-start(bf16[2,2,128,128]{3,2,1,0:T(8,128)(2,1)S(1)} %copy.51), channel_id=1, source_target_pairs={{0,4},{4,8},{8,12},{12,16},{16,20},{20,24},{24,28},{1,5},{5,9},{9,... | collective-permute-start | bytes 393224 | tf_op jit(solution)/shard_map/ppermute | solution.py:17
  131.3 7.2 %collective-permute-start.16 = (bf16[2,2,128,128]{3,2,1,0:T(8,128)(2,1)S(1)}, bf16[2,2,128,128]{3,2,1,0:T(8,128)(2,1)S(1)}, u32[]{:S(2)}, u32[]{:S(2)}) collective-permute-start(bf16[2,2,128,128]{3,2,1,0:T(8,128)(2,1)S(1)} %copy.51), channel_id=1, source_target_pairs={{4,0},{8,4},{12,8},{16,12},{20,16},{24,20},{28,24},{5,1},{9,5},{13... | collective-permute-start | bytes 393224 | tf_op jit(solution)/shard_map/ppermute | solution.py:18
  138.5 9.7 %collective-permute-start.18 = (bf16[2,6,128,128]{3,2,1,0:T(8,128)(2,1)S(1)}, bf16[2,6,128,128]{3,2,1,0:T(8,128)(2,1)S(1)}, u32[]{:S(2)}, u32[]{:S(2)}) collective-permute-start(bf16[2,6,128,128]{3,2,1,0:T(8,128)(2,1)S(1)} %constant_dynamic-update-slice_fusion.6), channel_id=1, source_target_pairs={{1,0},{2,1},{3,2},{5,4},{6,5},{7,6},{9,8},{10,9},{11,10},{13,12},{... | collective-permute-start | bytes 1179656 | tf_op jit(solution)/shard_map/ppermute | solution.py:18
  141.0 8.3 %collective-permute-start.17 = (bf16[2,6,128,128]{3,2,1,0:T(8,128)(2,1)S(1)}, bf16[2,6,128,128]{3,2,1,0:T(8,128)(2,1)S(1)}, u32[]{:S(2)}, u32[]{:S(2)}) collective-permute-start(bf16[2,6,128,128]{3,2,1,0:T(8,128)(2,1)S(1)} %constant_dynamic-update-slice_fusion.6), channel_id=1, source_target_pairs={{0,1},{1,2},{2,3},{4,5},{5,6},{6,7},{8,9},{9,10},{10,11},{12,13},{... | collective-permute-start | bytes 1179656 | tf_op jit(solution)/shard_map/ppermute | solution.py:17
  162.7 3.8 %collective-permute-start.19 = (bf16[256,128]{1,0:T(8,128)(2,1)S(1)}, bf16[256,128]{1,0:T(8,128)(2,1)S(1)}, u32[]{:S(2)}, u32[]{:S(2)}) collective-permute-start(bf16[256,128]{1,0:T(8,128)(2,1)S(1)} %bitcast.93), channel_id=1, source_target_pairs={{0,1},{1,2},{2,3},{4,5},{5,6},{6,7},{8,9},{9,10},{10,11},{12,13},{... | collective-permute-start | bytes 196616 | tf_op jit(solution)/shard_map/ppermute | solution.py:26
where the time goes:
time: 169 us; the launch traced here: 168 us
  starting transfers between devices  55.3 us (33%)
  blocking collectives  44.9 us (27%)
  waiting for transfers between devices  40.7 us (24%)
  matrix products  11.4 us (7%)
  local copies, waits for them, and re-layouts  9.57 us (6%)
  other arithmetic  5.1 us (3%)
    all_gather x4, blocking collectives, on_device(): lax.all_gather(loaded, 'vert', axis=0, tiled=True).astype(jnp.float32)  33.6 us
    ppermute x8, starting transfers between devices, extended(): before = lax.ppermute(last, axis, up)  30.4 us
    ppermute x8, waiting for transfers between devices, extended(): after = lax.ppermute(leading, axis, down)  25.3 us
    ppermute x8, starting transfers between devices, extended(): after = lax.ppermute(leading, axis, down)  14.9 us
    all_gather x1, blocking collectives, on_device(): all_columns = lax.all_gather(implicit_columns, 'vert', axis=0, tiled=True)  11.3 us
    ppermute x8, waiting for transfers between devices, extended(): before = lax.ppermute(last, axis, up)  10.7 us
    ppermute x4, starting transfers between devices, from_behind(): lax.ppermute(value, axis, [(source, source + steps) for source in range(l...  10 us
    dot_general x4, matrix products, on_device(): jnp.einsum('ltjab,ltjbs->ltas', explicit_tiles, picked, preferred_element...  6.59 us
  transfers between devices with their start and end apart: 20, of which 18 were waited for; matrix products, arithmetic and copies ran while one was open for 2% of the time, Pallas kernels for 0%

commit v1 on v0

--- a/solution.py
+++ b/solution.py
@@ -54,7 +54,15 @@
     source = surface_source.astype(jnp.float32)
     fall_rate = settling[None, None, :]
     wet_cells = wet_mask.astype(jnp.bfloat16)[:, :, None]
-    all_columns = lax.all_gather(implicit_columns, "vert", axis=0, tiled=True)
+    count_2 = lax.axis_size("vert")
+    current_2, tiles = (implicit_columns, [implicit_columns])
+    for _ in range(count_2 - 1):
+        current_2 = lax.ppermute(
+            current_2, "vert", [(i_2, (i_2 + 1) % count_2) for i_2 in range(count_2)]
+        )
+        tiles.insert(0, current_2)
+    merged = jnp.concatenate(tiles, axis=0)
+    all_columns = jnp.roll(merged, (lax.axis_index("vert") + 1) * implicit_columns.shape[0], axis=0)
     own_rows = lax.dynamic_slice_in_dim(all_columns, first_level, lev_dev, 1)
     current = tracer
     for step_index in range(STEPS):

time: 169 us -> 160 us (0.947)
  blocking collectives: 44.9 us -> 33.4 us
  starting transfers between devices: 55.3 us -> 61 us
  local copies, waits for them, and re-layouts: 9.57 us -> 6.21 us
  matrix products: 11.4 us -> 8.66 us
  other arithmetic: 5.1 us -> 7.45 us
    all_gather x1 -> x0, blocking collectives: 11.3 us -> none  [on_device(): all_columns = lax.all_gather(implicit_columns, 'vert', axis=0, tiled=True)]
    ppermute x0 -> x3, starting transfers between devices: none -> 5.45 us  [on_device(): lax.ppermute(current_2, 'vert', [(i_2, (i_2 + 1) % count_2) for i_2 in ra...]
    ppermute x0 -> x3, waiting for transfers between devices: none -> 3.99 us  [on_device(): lax.ppermute(current_2, 'vert', [(i_2, (i_2 + 1) % count_2) for i_2 in ra...]
    gather x4, local copies, waits for them, and re-layouts: 6.5 us -> 2.89 us  [on_device(): picked = flattened[position] * live_slots[:, :, :, None, None]]
    ppermute x8, waiting for transfers between devices: 25.3 us -> 21.9 us  [extended(): after = lax.ppermute(leading, axis, down)]
    dot_general x4, matrix products: 6.59 us -> 3.93 us  [on_device(): jnp.einsum('ltjab,ltjbs->ltas', explicit_tiles, picked, preferred_element...]
  transfers between devices with their start and end apart: 20 -> 23, of which waited for: 18 -> 19; matrix products, arithmetic and copies ran while one was open for 2% -> 4% of each run, Pallas kernels for 0% -> 0%
where the time goes in v1:
time: 160 us; the launch traced here: 159 us
  starting transfers between devices  61 us (38%)
  waiting for transfers between devices  41.4 us (26%)
  blocking collectives  33.4 us (21%)
  matrix products  8.66 us (5%)
  other arithmetic  7.45 us (5%)
  local copies, waits for them, and re-layouts  6.21 us (4%)
    all_gather x4, blocking collectives, on_device(): lax.all_gather(loaded, 'vert', axis=0, tiled=True).astype(jnp.float32)  33.4 us
    ppermute x8, starting transfers between devices, extended(): before = lax.ppermute(last, axis, up)  30.2 us
    ppermute x8, waiting for transfers between devices, extended(): after = lax.ppermute(leading, axis, down)  21.9 us
    ppermute x8, starting transfers between devices, extended(): after = lax.ppermute(leading, axis, down)  15.3 us
    ppermute x8, waiting for transfers between devices, extended(): before = lax.ppermute(last, axis, up)  10.8 us
    ppermute x4, starting transfers between devices, from_behind(): lax.ppermute(value, axis, [(source, source + steps) for source in range(l...  10 us
    ppermute x3, starting transfers between devices, on_device(): lax.ppermute(current_2, 'vert', [(i_2, (i_2 + 1) % count_2) for i_2 in ra...  5.45 us
    dot_general x4, matrix products, on_device(): jnp.einsum('ckm,mcs->kcs', own_rows, lax.all_gather(loaded, 'vert', axis=...  4.73 us
  transfers between devices with their start and end apart: 23, of which 19 were waited for; matrix products, arithmetic and copies ran while one was open for 4% of the time, Pallas kernels for 0%

profile of v1, /device:TPU:1, one launch (start us, length us, event | category | flops | bytes accessed | tf_op | source)
XLA Modules:
  0.0 158.7 jit_solution(13862008895483428939)
XLA Ops:
  1.4 4.6 %collective-permute-start = (bf16[2,2,128,128]{3,2,1,0:T(8,128)(2,1)}, bf16[2,2,128,128]{3,2,1,0:T(8,128)(2,1)S(1)}, u32[]{:S(2)}, u32[]{:S(2)}) collective-permute-start(bf16[2,2,128,128]{3,2,1,0:T(8,128)(2,1)} %bitcast.87), channel_id=1, source_target_pairs={{0,4},{4,8},{8,12},{12,16},{16,20},{20,24},{24,28},{1,5},{5,9},{9,... | collective-permute-start | bytes 393224 | tf_op jit(solution)/shard_map/ppermute | solution.py:17
  6.0 2.6 %collective-permute-start.4 = (f32[64,8,8]{0,2,1:T(8,128)}, f32[64,8,8]{0,2,1:T(8,128)S(1)}, u32[]{:S(2)}, u32[]{:S(2)}) collective-permute-start(f32[64,8,8]{0,2,1:T(8,128)} %param.13), channel_id=1, source_target_pairs={{0,1},{1,2},{2,3},{3,0},{4,5},{5,6},{6,7},{7,4},{8,9},{9,10},{10,1... | collective-permute-start | bytes 49160 | tf_op jit(solution)/shard_map/ppermute | solution.py:60
  12.3 2.4 %collective-permute-start.3 = (bf16[2,6,128,128]{3,2,1,0:T(8,128)(2,1)S(1)}, bf16[2,6,128,128]{3,2,1,0:T(8,128)(2,1)S(1)}, u32[]{:S(2)}, u32[]{:S(2)}) collective-permute-start(bf16[2,6,128,128]{3,2,1,0:T(8,128)(2,1)S(1)} %pad_maximum_fusion.4), channel_id=1, source_target_pairs={{1,0},{2,1},{3,2},{5,4},{6,5},{7,6},{9,8},{10,9},{11,10},{13,12},{... | collective-permute-start | bytes 1179656 | tf_op jit(solution)/shard_map/ppermute | solution.py:18
  14.7 3.2 %collective-permute-start.2 = (bf16[2,6,128,128]{3,2,1,0:T(8,128)(2,1)S(1)}, bf16[2,6,128,128]{3,2,1,0:T(8,128)(2,1)}, u32[]{:S(2)}, u32[]{:S(2)}) collective-permute-start(bf16[2,6,128,128]{3,2,1,0:T(8,128)(2,1)S(1)} %pad_maximum_fusion.4), channel_id=1, source_target_pairs={{0,1},{1,2},{2,3},{4,5},{5,6},{6,7},{8,9},{9,10},{10,11},{12,13},{... | collective-permute-start | bytes 1179656 | tf_op jit(solution)/shard_map/ppermute | solution.py:17
  19.1 3.8 %collective-permute-done.5 = f32[64,8,8]{0,2,1:T(8,128)S(1)} collective-permute-done((f32[64,8,8]{0,2,1:T(8,128)S(1)}, f32[64,8,8]{0,2,1:T(8,128)S(1)}, u32[]{:S(2)}, u32[]{:S(2)}) %collective-permute-start.5) | collective-permute-done | bytes 16416 | tf_op jit(solution)/shard_map/ppermute | solution.py:60
  22.9 2.5 %collective-permute-start.6 = (f32[64,8,8]{0,2,1:T(8,128)S(1)}, f32[64,8,8]{0,2,1:T(8,128)S(1)}, u32[]{:S(2)}, u32[]{:S(2)}) collective-permute-start(f32[64,8,8]{0,2,1:T(8,128)S(1)} %collective-permute-done.5), channel_id=1, source_target_pairs={{0,1},{1,2},{2,3},{3,0},{4,5},{5,6},{6,7},{7,4},{8,9},{9,10},{10,1... | collective-permute-start | bytes 49160 | tf_op jit(solution)/shard_map/ppermute | solution.py:60
  30.1 8.2 %all_gather.12 = bf16[8,256,128]{2,1,0:T(8,128)(2,1)S(1)} all-gather(bf16[2,256,128]{2,1,0:T(8,128)(2,1)S(1)} %fusion.16), channel_id=1, replica_groups=mesh['horiz'=8,'vert'=4] {'vert'}, dimensions={0}, use_global_device_ids=true | all-gather | bytes 655360 | tf_op jit(solution)/shard_map/all_gather | solution.py:82
  39.7 2.5 %collective-permute-start.7 = (bf16[256,128]{1,0:T(8,128)(2,1)S(1)}, bf16[256,128]{1,0:T(8,128)(2,1)S(1)}, u32[]{:S(2)}, u32[]{:S(2)}) collective-permute-start(bf16[256,128]{1,0:T(8,128)(2,1)S(1)} %bitcast.94), channel_id=1, source_target_pairs={{0,1},{1,2},{2,3},{4,5},{5,6},{6,7},{8,9},{9,10},{10,11},{12,13},{... | collective-permute-start | bytes 196616 | tf_op jit(solution)/shard_map/ppermute | solution.py:26
  44.0 4.0 %collective-permute-start.8 = (bf16[2,2,128,128]{3,2,1,0:T(8,128)(2,1)S(1)}, bf16[2,2,128,128]{3,2,1,0:T(8,128)(2,1)S(1)}, u32[]{:S(2)}, u32[]{:S(2)}) collective-permute-start(bf16[2,2,128,128]{3,2,1,0:T(8,128)(2,1)S(1)} %copy.46), channel_id=1, source_target_pairs={{0,4},{4,8},{8,12},{12,16},{16,20},{20,24},{24,28},{1,5},{5,9},{9,... | collective-permute-start | bytes 393224 | tf_op jit(solution)/shard_map/ppermute | solution.py:17
  49.3 2.0 %collective-permute-done.8 = bf16[2,2,128,128]{3,2,1,0:T(8,128)(2,1)S(1)} collective-permute-done((bf16[2,2,128,128]{3,2,1,0:T(8,128)(2,1)S(1)}, bf16[2,2,128,128]{3,2,1,0:T(8,128)(2,1)S(1)}, u32[]{:S(2)}, u32[]{:S(2)}) %collective-permute-start.8) | collective-permute-done | bytes 131104 | tf_op jit(solution)/shard_map/ppermute | solution.py:17
  51.3 3.8 %collective-permute-done.9 = bf16[2,2,128,128]{3,2,1,0:T(8,128)(2,1)S(1)} collective-permute-done((bf16[2,2,128,128]{3,2,1,0:T(8,128)(2,1)S(1)}, bf16[2,2,128,128]{3,2,1,0:T(8,128)(2,1)S(1)}, u32[]{:S(2)}, u32[]{:S(2)}) %collective-permute-start.9) | collective-permute-done | bytes 131104 | tf_op jit(solution)/shard_map/ppermute | solution.py:18
  55.2 2.5 %collective-permute-start.11 = (bf16[2,6,128,128]{3,2,1,0:T(8,128)(2,1)S(1)}, bf16[2,6,128,128]{3,2,1,0:T(8,128)(2,1)S(1)}, u32[]{:S(2)}, u32[]{:S(2)}) collective-permute-start(bf16[2,6,128,128]{3,2,1,0:T(8,128)(2,1)S(1)} %constant_dynamic-update-slice_fusion), channel_id=1, source_target_pairs={{1,0},{2,1},{3,2},{5,4},{6,5},{7,6},{9,8},{10,9},{11,10},{13,12},{... | collective-permute-start | bytes 1179656 | tf_op jit(solution)/shard_map/ppermute | solution.py:18
  57.7 3.6 %collective-permute-start.10 = (bf16[2,6,128,128]{3,2,1,0:T(8,128)(2,1)S(1)}, bf16[2,6,128,128]{3,2,1,0:T(8,128)(2,1)S(1)}, u32[]{:S(2)}, u32[]{:S(2)}) collective-permute-start(bf16[2,6,128,128]{3,2,1,0:T(8,128)(2,1)S(1)} %constant_dynamic-update-slice_fusion), channel_id=1, source_target_pairs={{0,1},{1,2},{2,3},{4,5},{5,6},{6,7},{8,9},{9,10},{10,11},{12,13},{... | collective-permute-start | bytes 1179656 | tf_op jit(solution)/shard_map/ppermute | solution.py:17
  61.4 3.5 %collective-permute-done.11 = bf16[2,6,128,128]{3,2,1,0:T(8,128)(2,1)S(1)} collective-permute-done((bf16[2,6,128,128]{3,2,1,0:T(8,128)(2,1)S(1)}, bf16[2,6,128,128]{3,2,1,0:T(8,128)(2,1)S(1)}, u32[]{:S(2)}, u32[]{:S(2)}) %collective-permute-start.11) | collective-permute-done | bytes 393248 | tf_op jit(solution)/shard_map/ppermute | solution.py:18
  68.2 8.4 %all_gather.13 = bf16[8,256,128]{2,1,0:T(8,128)(2,1)S(1)} all-gather(bf16[2,256,128]{2,1,0:T(8,128)(2,1)S(1)} %fusion.17), channel_id=1, replica_groups=mesh['horiz'=8,'vert'=4] {'vert'}, dimensions={0}, use_global_device_ids=true | all-gather | bytes 655360 | tf_op jit(solution)/shard_map/all_gather | solution.py:82
  77.9 2.5 %collective-permute-start.12 = (bf16[256,128]{1,0:T(8,128)(2,1)S(1)}, bf16[256,128]{1,0:T(8,128)(2,1)S(1)}, u32[]{:S(2)}, u32[]{:S(2)}) collective-permute-start(bf16[256,128]{1,0:T(8,128)(2,1)S(1)} %bitcast.95), channel_id=1, source_target_pairs={{0,1},{1,2},{2,3},{4,5},{5,6},{6,7},{8,9},{9,10},{10,11},{12,13},{... | collective-permute-start | bytes 196616 | tf_op jit(solution)/shard_map/ppermute | solution.py:26
  82.2 4.2 %collective-permute-start.13 = (bf16[2,2,128,128]{3,2,1,0:T(8,128)(2,1)S(1)}, bf16[2,2,128,128]{3,2,1,0:T(8,128)(2,1)S(1)}, u32[]{:S(2)}, u32[]{:S(2)}) collective-permute-start(bf16[2,2,128,128]{3,2,1,0:T(8,128)(2,1)S(1)} %copy.51), channel_id=1, source_target_pairs={{0,4},{4,8},{8,12},{12,16},{16,20},{20,24},{24,28},{1,5},{5,9},{9,... | collective-permute-start | bytes 393224 | tf_op jit(solution)/shard_map/ppermute | solution.py:17
  87.6 2.0 %collective-permute-done.13 = bf16[2,2,128,128]{3,2,1,0:T(8,128)(2,1)S(1)} collective-permute-done((bf16[2,2,128,128]{3,2,1,0:T(8,128)(2,1)S(1)}, bf16[2,2,128,128]{3,2,1,0:T(8,128)(2,1)S(1)}, u32[]{:S(2)}, u32[]{:S(2)}) %collective-permute-start.13) | collective-permute-done | bytes 131104 | tf_op jit(solution)/shard_map/ppermute | solution.py:17
  89.7 3.8 %collective-permute-done.14 = bf16[2,2,128,128]{3,2,1,0:T(8,128)(2,1)S(1)} collective-permute-done((bf16[2,2,128,128]{3,2,1,0:T(8,128)(2,1)S(1)}, bf16[2,2,128,128]{3,2,1,0:T(8,128)(2,1)S(1)}, u32[]{:S(2)}, u32[]{:S(2)}) %collective-permute-start.14) | collective-permute-done | bytes 131104 | tf_op jit(solution)/shard_map/ppermute | solution.py:18
  93.5 2.5 %collective-permute-start.16 = (bf16[2,6,128,128]{3,2,1,0:T(8,128)(2,1)S(1)}, bf16[2,6,128,128]{3,2,1,0:T(8,128)(2,1)S(1)}, u32[]{:S(2)}, u32[]{:S(2)}) collective-permute-start(bf16[2,6,128,128]{3,2,1,0:T(8,128)(2,1)S(1)} %constant_dynamic-update-slice_fusion.3), channel_id=1, source_target_pairs={{1,0},{2,1},{3,2},{5,4},{6,5},{7,6},{9,8},{10,9},{11,10},{13,12},{... | collective-permute-start | bytes 1179656 | tf_op jit(solution)/shard_map/ppermute | solution.py:18
  96.1 3.6 %collective-permute-start.15 = (bf16[2,6,128,128]{3,2,1,0:T(8,128)(2,1)S(1)}, bf16[2,6,128,128]{3,2,1,0:T(8,128)(2,1)S(1)}, u32[]{:S(2)}, u32[]{:S(2)}) collective-permute-start(bf16[2,6,128,128]{3,2,1,0:T(8,128)(2,1)S(1)} %constant_dynamic-update-slice_fusion.3), channel_id=1, source_target_pairs={{0,1},{1,2},{2,3},{4,5},{5,6},{6,7},{8,9},{9,10},{10,11},{12,13},{... | collective-permute-start | bytes 1179656 | tf_op jit(solution)/shard_map/ppermute | solution.py:17
  99.7 3.5 %collective-permute-done.16 = bf16[2,6,128,128]{3,2,1,0:T(8,128)(2,1)S(1)} collective-permute-done((bf16[2,6,128,128]{3,2,1,0:T(8,128)(2,1)S(1)}, bf16[2,6,128,128]{3,2,1,0:T(8,128)(2,1)S(1)}, u32[]{:S(2)}, u32[]{:S(2)}) %collective-permute-start.16) | collective-permute-done | bytes 393248 | tf_op jit(solution)/shard_map/ppermute | solution.py:18
  106.5 8.4 %all_gather.14 = bf16[8,256,128]{2,1,0:T(8,128)(2,1)S(1)} all-gather(bf16[2,256,128]{2,1,0:T(8,128)(2,1)S(1)} %fusion.18), channel_id=1, replica_groups=mesh['horiz'=8,'vert'=4] {'vert'}, dimensions={0}, use_global_device_ids=true | all-gather | bytes 655360 | tf_op jit(solution)/shard_map/all_gather | solution.py:82
  116.3 2.5 %collective-permute-start.17 = (bf16[256,128]{1,0:T(8,128)(2,1)S(1)}, bf16[256,128]{1,0:T(8,128)(2,1)S(1)}, u32[]{:S(2)}, u32[]{:S(2)}) collective-permute-start(bf16[256,128]{1,0:T(8,128)(2,1)S(1)} %bitcast.96), channel_id=1, source_target_pairs={{0,1},{1,2},{2,3},{4,5},{5,6},{6,7},{8,9},{9,10},{10,11},{12,13},{... | collective-permute-start | bytes 196616 | tf_op jit(solution)/shard_map/ppermute | solution.py:26
  120.5 3.3 %collective-permute-start.18 = (bf16[2,2,128,128]{3,2,1,0:T(8,128)(2,1)S(1)}, bf16[2,2,128,128]{3,2,1,0:T(8,128)(2,1)S(1)}, u32[]{:S(2)}, u32[]{:S(2)}) collective-permute-start(bf16[2,2,128,128]{3,2,1,0:T(8,128)(2,1)S(1)} %copy.55), channel_id=1, source_target_pairs={{0,4},{4,8},{8,12},{12,16},{16,20},{20,24},{24,28},{1,5},{5,9},{9,... | collective-permute-start | bytes 393224 | tf_op jit(solution)/shard_map/ppermute | solution.py:17
  125.1 2.0 %collective-permute-done.18 = bf16[2,2,128,128]{3,2,1,0:T(8,128)(2,1)S(1)} collective-permute-done((bf16[2,2,128,128]{3,2,1,0:T(8,128)(2,1)S(1)}, bf16[2,2,128,128]{3,2,1,0:T(8,128)(2,1)S(1)}, u32[]{:S(2)}, u32[]{:S(2)}) %collective-permute-start.18) | collective-permute-done | bytes 131104 | tf_op jit(solution)/shard_map/ppermute | solution.py:17
  127.2 3.8 %collective-permute-done.19 = bf16[2,2,128,128]{3,2,1,0:T(8,128)(2,1)S(1)} collective-permute-done((bf16[2,2,128,128]{3,2,1,0:T(8,128)(2,1)S(1)}, bf16[2,2,128,128]{3,2,1,0:T(8,128)(2,1)S(1)}, u32[]{:S(2)}, u32[]{:S(2)}) %collective-permute-start.19) | collective-permute-done | bytes 131104 | tf_op jit(solution)/shard_map/ppermute | solution.py:18
  131.0 2.5 %collective-permute-start.21 = (bf16[2,6,128,128]{3,2,1,0:T(8,128)(2,1)S(1)}, bf16[2,6,128,128]{3,2,1,0:T(8,128)(2,1)S(1)}, u32[]{:S(2)}, u32[]{:S(2)}) collective-permute-start(bf16[2,6,128,128]{3,2,1,0:T(8,128)(2,1)S(1)} %constant_dynamic-update-slice_fusion.6), channel_id=1, source_target_pairs={{1,0},{2,1},{3,2},{5,4},{6,5},{7,6},{9,8},{10,9},{11,10},{13,12},{... | collective-permute-start | bytes 1179656 | tf_op jit(solution)/shard_map/ppermute | solution.py:18
  133.6 3.8 %collective-permute-start.20 = (bf16[2,6,128,128]{3,2,1,0:T(8,128)(2,1)S(1)}, bf16[2,6,128,128]{3,2,1,0:T(8,128)(2,1)S(1)}, u32[]{:S(2)}, u32[]{:S(2)}) collective-permute-start(bf16[2,6,128,128]{3,2,1,0:T(8,128)(2,1)S(1)} %constant_dynamic-update-slice_fusion.6), channel_id=1, source_target_pairs={{0,1},{1,2},{2,3},{4,5},{5,6},{6,7},{8,9},{9,10},{10,11},{12,13},{... | collective-permute-start | bytes 1179656 | tf_op jit(solution)/shard_map/ppermute | solution.py:17
  137.4 3.3 %collective-permute-done.21 = bf16[2,6,128,128]{3,2,1,0:T(8,128)(2,1)S(1)} collective-permute-done((bf16[2,6,128,128]{3,2,1,0:T(8,128)(2,1)S(1)}, bf16[2,6,128,128]{3,2,1,0:T(8,128)(2,1)S(1)}, u32[]{:S(2)}, u32[]{:S(2)}) %collective-permute-start.21) | collective-permute-done | bytes 393248 | tf_op jit(solution)/shard_map/ppermute | solution.py:18
  144.0 8.4 %all_gather.15 = bf16[8,256,128]{2,1,0:T(8,128)(2,1)S(1)} all-gather(bf16[2,256,128]{2,1,0:T(8,128)(2,1)S(1)} %fusion.19), channel_id=1, replica_groups=mesh['horiz'=8,'vert'=4] {'vert'}, dimensions={0}, use_global_device_ids=true | all-gather | bytes 655360 | tf_op jit(solution)/shard_map/all_gather | solution.py:82
  153.8 2.5 %collective-permute-start.22 = (bf16[256,128]{1,0:T(8,128)(2,1)S(1)}, bf16[256,128]{1,0:T(8,128)(2,1)S(1)}, u32[]{:S(2)}, u32[]{:S(2)}) collective-permute-start(bf16[256,128]{1,0:T(8,128)(2,1)S(1)} %bitcast.97), channel_id=1, source_target_pairs={{0,1},{1,2},{2,3},{4,5},{5,6},{6,7},{8,9},{9,10},{10,11},{12,13},{... | collective-permute-start | bytes 196616 | tf_op jit(solution)/shard_map/ppermute | solution.py:26
  (92 shorter events, 37.7 us)
Async XLA Ops:
  0.0 29.5 %copy-start = (bf16[2,2,7,128,128]{4,3,2,1,0:T(8,128)(2,1)S(1)}, bf16[2,2,7,128,128]{4,3,2,1,0:T(8,128)(2,1)}, u32[]{:S(2)}) copy-start(bf16[2,2,7,128,128]{4,3,2,1,0:T(8,128)(2,1)} %param.9) | copy-start | bytes 2752516
  0.0 27.6 %copy-start.1 = (bf16[2,256,128]{2,1,0:T(8,128)(2,1)S(1)}, bf16[2,256,128]{2,1,0:T(8,128)(2,1)}, u32[]{:S(2)}) copy-start(bf16[2,256,128]{2,1,0:T(8,128)(2,1)} %param.8) | copy-start | bytes 393220
  0.0 10.0 %collective-permute-start.1 = (bf16[2,2,128,128]{3,2,1,0:T(8,128)(2,1)}, bf16[2,2,128,128]{3,2,1,0:T(8,128)(2,1)S(1)}, u32[]{:S(2)}, u32[]{:S(2)}) collective-permute-start(bf16[2,2,128,128]{3,2,1,0:T(8,128)(2,1)} %bitcast.86), channel_id=1, source_target_pairs={{4,0},{8,4},{12,8},{16,12},{20,16},{24,20},{28,24},{5,1},{9,5},{13... | collective-permute-start | bytes 393224 | tf_op jit(solution)/shard_map/ppermute | solution.py:18
  1.4 9.9 %collective-permute-start = (bf16[2,2,128,128]{3,2,1,0:T(8,128)(2,1)}, bf16[2,2,128,128]{3,2,1,0:T(8,128)(2,1)S(1)}, u32[]{:S(2)}, u32[]{:S(2)}) collective-permute-start(bf16[2,2,128,128]{3,2,1,0:T(8,128)(2,1)} %bitcast.87), channel_id=1, source_target_pairs={{0,4},{4,8},{8,12},{12,16},{16,20},{20,24},{24,28},{1,5},{5,9},{9,... | collective-permute-start | bytes 393224 | tf_op jit(solution)/shard_map/ppermute | solution.py:17
  6.0 12.7 %collective-permute-start.4 = (f32[64,8,8]{0,2,1:T(8,128)}, f32[64,8,8]{0,2,1:T(8,128)S(1)}, u32[]{:S(2)}, u32[]{:S(2)}) collective-permute-start(f32[64,8,8]{0,2,1:T(8,128)} %param.13), channel_id=1, source_target_pairs={{0,1},{1,2},{2,3},{3,0},{4,5},{5,6},{6,7},{7,4},{8,9},{9,10},{10,1... | collective-permute-start | bytes 49160 | tf_op jit(solution)/shard_map/ppermute | solution.py:60
  12.3 15.3 %collective-permute-start.3 = (bf16[2,6,128,128]{3,2,1,0:T(8,128)(2,1)S(1)}, bf16[2,6,128,128]{3,2,1,0:T(8,128)(2,1)S(1)}, u32[]{:S(2)}, u32[]{:S(2)}) collective-permute-start(bf16[2,6,128,128]{3,2,1,0:T(8,128)(2,1)S(1)} %pad_maximum_fusion.4), channel_id=1, source_target_pairs={{1,0},{2,1},{3,2},{5,4},{6,5},{7,6},{9,8},{10,9},{11,10},{13,12},{... | collective-permute-start | bytes 1179656 | tf_op jit(solution)/shard_map/ppermute | solution.py:18
  14.7 12.9 %collective-permute-start.2 = (bf16[2,6,128,128]{3,2,1,0:T(8,128)(2,1)S(1)}, bf16[2,6,128,128]{3,2,1,0:T(8,128)(2,1)}, u32[]{:S(2)}, u32[]{:S(2)}) collective-permute-start(bf16[2,6,128,128]{3,2,1,0:T(8,128)(2,1)S(1)} %pad_maximum_fusion.4), channel_id=1, source_target_pairs={{0,1},{1,2},{2,3},{4,5},{5,6},{6,7},{8,9},{9,10},{10,11},{12,13},{... | collective-permute-start | bytes 1179656 | tf_op jit(solution)/shard_map/ppermute | solution.py:17
  18.6 11.4 %copy-start.3 = (bf16[2,2,7]{2,1,0:T(2,128)(2,1)}, bf16[2,2,7]{2,1,0:T(2,128)(2,1)S(1)}, u32[]{:S(2)}) copy-start(bf16[2,2,7]{2,1,0:T(2,128)(2,1)S(1)} %compare_convert_fusion) | copy-start | bytes 172
  18.7 4.2 %collective-permute-start.5 = (f32[64,8,8]{0,2,1:T(8,128)S(1)}, f32[64,8,8]{0,2,1:T(8,128)S(1)}, u32[]{:S(2)}, u32[]{:S(2)}) collective-permute-start(f32[64,8,8]{0,2,1:T(8,128)S(1)} %collective-permute-done.4), channel_id=1, source_target_pairs={{0,1},{1,2},{2,3},{3,0},{4,5},{5,6},{6,7},{7,4},{8,9},{9,10},{10,1... | collective-permute-start | bytes 49160 | tf_op jit(solution)/shard_map/ppermute | solution.py:60
  22.9 3.5 %collective-permute-start.6 = (f32[64,8,8]{0,2,1:T(8,128)S(1)}, f32[64,8,8]{0,2,1:T(8,128)S(1)}, u32[]{:S(2)}, u32[]{:S(2)}) collective-permute-start(f32[64,8,8]{0,2,1:T(8,128)S(1)} %collective-permute-done.5), channel_id=1, source_target_pairs={{0,1},{1,2},{2,3},{3,0},{4,5},{5,6},{6,7},{7,4},{8,9},{9,10},{10,1... | collective-permute-start | bytes 49160 | tf_op jit(solution)/shard_map/ppermute | solution.py:60
  30.1 12.1 %copy-start.2 = (f32[128]{0:T(128)S(1)}, f32[128]{0:T(128)}, u32[]{:S(2)}) copy-start(f32[128]{0:T(128)} %param.14) | copy-start | bytes 1540
  39.7 3.8 %collective-permute-start.7 = (bf16[256,128]{1,0:T(8,128)(2,1)S(1)}, bf16[256,128]{1,0:T(8,128)(2,1)S(1)}, u32[]{:S(2)}, u32[]{:S(2)}) collective-permute-start(bf16[256,128]{1,0:T(8,128)(2,1)S(1)} %bitcast.94), channel_id=1, source_target_pairs={{0,1},{1,2},{2,3},{4,5},{5,6},{6,7},{8,9},{9,10},{10,11},{12,13},{... | collective-permute-start | bytes 196616 | tf_op jit(solution)/shard_map/ppermute | solution.py:26
  44.0 7.3 %collective-permute-start.8 = (bf16[2,2,128,128]{3,2,1,0:T(8,128)(2,1)S(1)}, bf16[2,2,128,128]{3,2,1,0:T(8,128)(2,1)S(1)}, u32[]{:S(2)}, u32[]{:S(2)}) collective-permute-start(bf16[2,2,128,128]{3,2,1,0:T(8,128)(2,1)S(1)} %copy.46), channel_id=1, source_target_pairs={{0,4},{4,8},{8,12},{12,16},{16,20},{20,24},{24,28},{1,5},{5,9},{9,... | collective-permute-start | bytes 393224 | tf_op jit(solution)/shard_map/ppermute | solution.py:17
  48.0 7.2 %collective-permute-start.9 = (bf16[2,2,128,128]{3,2,1,0:T(8,128)(2,1)S(1)}, bf16[2,2,128,128]{3,2,1,0:T(8,128)(2,1)S(1)}, u32[]{:S(2)}, u32[]{:S(2)}) collective-permute-start(bf16[2,2,128,128]{3,2,1,0:T(8,128)(2,1)S(1)} %copy.46), channel_id=1, source_target_pairs={{4,0},{8,4},{12,8},{16,12},{20,16},{24,20},{28,24},{5,1},{9,5},{13... | collective-permute-start | bytes 393224 | tf_op jit(solution)/shard_map/ppermute | solution.py:18
  55.2 9.7 %collective-permute-start.11 = (bf16[2,6,128,128]{3,2,1,0:T(8,128)(2,1)S(1)}, bf16[2,6,128,128]{3,2,1,0:T(8,128)(2,1)S(1)}, u32[]{:S(2)}, u32[]{:S(2)}) collective-permute-start(bf16[2,6,128,128]{3,2,1,0:T(8,128)(2,1)S(1)} %constant_dynamic-update-slice_fusion), channel_id=1, source_target_pairs={{1,0},{2,1},{3,2},{5,4},{6,5},{7,6},{9,8},{10,9},{11,10},{13,12},{... | collective-permute-start | bytes 1179656 | tf_op jit(solution)/shard_map/ppermute | solution.py:18
  57.7 8.3 %collective-permute-start.10 = (bf16[2,6,128,128]{3,2,1,0:T(8,128)(2,1)S(1)}, bf16[2,6,128,128]{3,2,1,0:T(8,128)(2,1)S(1)}, u32[]{:S(2)}, u32[]{:S(2)}) collective-permute-start(bf16[2,6,128,128]{3,2,1,0:T(8,128)(2,1)S(1)} %constant_dynamic-update-slice_fusion), channel_id=1, source_target_pairs={{0,1},{1,2},{2,3},{4,5},{5,6},{6,7},{8,9},{9,10},{10,11},{12,13},{... | collective-permute-start | bytes 1179656 | tf_op jit(solution)/shard_map/ppermute | solution.py:17
  77.9 3.8 %collective-permute-start.12 = (bf16[256,128]{1,0:T(8,128)(2,1)S(1)}, bf16[256,128]{1,0:T(8,128)(2,1)S(1)}, u32[]{:S(2)}, u32[]{:S(2)}) collective-permute-start(bf16[256,128]{1,0:T(8,128)(2,1)S(1)} %bitcast.95), channel_id=1, source_target_pairs={{0,1},{1,2},{2,3},{4,5},{5,6},{6,7},{8,9},{9,10},{10,11},{12,13},{... | collective-permute-start | bytes 196616 | tf_op jit(solution)/shard_map/ppermute | solution.py:26
  82.2 7.4 %collective-permute-start.13 = (bf16[2,2,128,128]{3,2,1,0:T(8,128)(2,1)S(1)}, bf16[2,2,128,128]{3,2,1,0:T(8,128)(2,1)S(1)}, u32[]{:S(2)}, u32[]{:S(2)}) collective-permute-start(bf16[2,2,128,128]{3,2,1,0:T(8,128)(2,1)S(1)} %copy.51), channel_id=1, source_target_pairs={{0,4},{4,8},{8,12},{12,16},{16,20},{20,24},{24,28},{1,5},{5,9},{9,... | collective-permute-start | bytes 393224 | tf_op jit(solution)/shard_map/ppermute | solution.py:17
  86.3 7.2 %collective-permute-start.14 = (bf16[2,2,128,128]{3,2,1,0:T(8,128)(2,1)S(1)}, bf16[2,2,128,128]{3,2,1,0:T(8,128)(2,1)S(1)}, u32[]{:S(2)}, u32[]{:S(2)}) collective-permute-start(bf16[2,2,128,128]{3,2,1,0:T(8,128)(2,1)S(1)} %copy.51), channel_id=1, source_target_pairs={{4,0},{8,4},{12,8},{16,12},{20,16},{24,20},{28,24},{5,1},{9,5},{13... | collective-permute-start | bytes 393224 | tf_op jit(solution)/shard_map/ppermute | solution.py:18
  93.5 9.7 %collective-permute-start.16 = (bf16[2,6,128,128]{3,2,1,0:T(8,128)(2,1)S(1)}, bf16[2,6,128,128]{3,2,1,0:T(8,128)(2,1)S(1)}, u32[]{:S(2)}, u32[]{:S(2)}) collective-permute-start(bf16[2,6,128,128]{3,2,1,0:T(8,128)(2,1)S(1)} %constant_dynamic-update-slice_fusion.3), channel_id=1, source_target_pairs={{1,0},{2,1},{3,2},{5,4},{6,5},{7,6},{9,8},{10,9},{11,10},{13,12},{... | collective-permute-start | bytes 1179656 | tf_op jit(solution)/shard_map/ppermute | solution.py:18
  96.1 8.3 %collective-permute-start.15 = (bf16[2,6,128,128]{3,2,1,0:T(8,128)(2,1)S(1)}, bf16[2,6,128,128]{3,2,1,0:T(8,128)(2,1)S(1)}, u32[]{:S(2)}, u32[]{:S(2)}) collective-permute-start(bf16[2,6,128,128]{3,2,1,0:T(8,128)(2,1)S(1)} %constant_dynamic-update-slice_fusion.3), channel_id=1, source_target_pairs={{0,1},{1,2},{2,3},{4,5},{5,6},{6,7},{8,9},{9,10},{10,11},{12,13},{... | collective-permute-start | bytes 1179656 | tf_op jit(solution)/shard_map/ppermute | solution.py:17
  116.3 3.8 %collective-permute-start.17 = (bf16[256,128]{1,0:T(8,128)(2,1)S(1)}, bf16[256,128]{1,0:T(8,128)(2,1)S(1)}, u32[]{:S(2)}, u32[]{:S(2)}) collective-permute-start(bf16[256,128]{1,0:T(8,128)(2,1)S(1)} %bitcast.96), channel_id=1, source_target_pairs={{0,1},{1,2},{2,3},{4,5},{5,6},{6,7},{8,9},{9,10},{10,11},{12,13},{... | collective-permute-start | bytes 196616 | tf_op jit(solution)/shard_map/ppermute | solution.py:26
  120.5 6.6 %collective-permute-start.18 = (bf16[2,2,128,128]{3,2,1,0:T(8,128)(2,1)S(1)}, bf16[2,2,128,128]{3,2,1,0:T(8,128)(2,1)S(1)}, u32[]{:S(2)}, u32[]{:S(2)}) collective-permute-start(bf16[2,2,128,128]{3,2,1,0:T(8,128)(2,1)S(1)} %copy.55), channel_id=1, source_target_pairs={{0,4},{4,8},{8,12},{12,16},{16,20},{20,24},{24,28},{1,5},{5,9},{9,... | collective-permute-start | bytes 393224 | tf_op jit(solution)/shard_map/ppermute | solution.py:17
  123.8 7.2 %collective-permute-start.19 = (bf16[2,2,128,128]{3,2,1,0:T(8,128)(2,1)S(1)}, bf16[2,2,128,128]{3,2,1,0:T(8,128)(2,1)S(1)}, u32[]{:S(2)}, u32[]{:S(2)}) collective-permute-start(bf16[2,2,128,128]{3,2,1,0:T(8,128)(2,1)S(1)} %copy.55), channel_id=1, source_target_pairs={{4,0},{8,4},{12,8},{16,12},{20,16},{24,20},{28,24},{5,1},{9,5},{13... | collective-permute-start | bytes 393224 | tf_op jit(solution)/shard_map/ppermute | solution.py:18
  131.0 9.7 %collective-permute-start.21 = (bf16[2,6,128,128]{3,2,1,0:T(8,128)(2,1)S(1)}, bf16[2,6,128,128]{3,2,1,0:T(8,128)(2,1)S(1)}, u32[]{:S(2)}, u32[]{:S(2)}) collective-permute-start(bf16[2,6,128,128]{3,2,1,0:T(8,128)(2,1)S(1)} %constant_dynamic-update-slice_fusion.6), channel_id=1, source_target_pairs={{1,0},{2,1},{3,2},{5,4},{6,5},{7,6},{9,8},{10,9},{11,10},{13,12},{... | collective-permute-start | bytes 1179656 | tf_op jit(solution)/shard_map/ppermute | solution.py:18
  133.6 8.3 %collective-permute-start.20 = (bf16[2,6,128,128]{3,2,1,0:T(8,128)(2,1)S(1)}, bf16[2,6,128,128]{3,2,1,0:T(8,128)(2,1)S(1)}, u32[]{:S(2)}, u32[]{:S(2)}) collective-permute-start(bf16[2,6,128,128]{3,2,1,0:T(8,128)(2,1)S(1)} %constant_dynamic-update-slice_fusion.6), channel_id=1, source_target_pairs={{0,1},{1,2},{2,3},{4,5},{5,6},{6,7},{8,9},{9,10},{10,11},{12,13},{... | collective-permute-start | bytes 1179656 | tf_op jit(solution)/shard_map/ppermute | solution.py:17
  153.8 3.8 %collective-permute-start.22 = (bf16[256,128]{1,0:T(8,128)(2,1)S(1)}, bf16[256,128]{1,0:T(8,128)(2,1)S(1)}, u32[]{:S(2)}, u32[]{:S(2)}) collective-permute-start(bf16[256,128]{1,0:T(8,128)(2,1)S(1)} %bitcast.97), channel_id=1, source_target_pairs={{0,1},{1,2},{2,3},{4,5},{5,6},{6,7},{8,9},{9,10},{10,11},{12,13},{... | collective-permute-start | bytes 196616 | tf_op jit(solution)/shard_map/ppermute | solution.py:26
